TPU v7x, 32 devices: a whole 2x2x4 slice. The times are simulated.
32 devices in a mesh: seq: 4 (over z), head: 8 (over y, x, core).
Axes of the slice: x: 2, y: 2, z: 4, core: 2. Of those that a mesh axis runs over, the one named last changes fastest.
Arguments:
- tokens: bfloat16 [4096, 4096], P(('seq', 'head')), may hold values from -6 to 6
- doc_lengths: int32 [16], replicated, may hold values from 1 to 2560, as said below
- value_weight: bfloat16 [4096, 8192], P('seq', 'head'), may hold values from -0.09375 to 0.09375
- gate_weight: bfloat16 [4096, 8192], P('seq', 'head'), may hold values from -0.09375 to 0.09375
- state_weight: bfloat16 [8, 4096, 256], P(None, 'seq'), may hold values from -0.09375 to 0.09375
- step_weight: bfloat16 [4096, 128], P('seq', 'head'), may hold values from -0.09375 to 0.09375
- value_conv: float32 [4, 8192], P(None, 'head'), may hold values from -3 to 3
- state_conv: float32 [8, 4, 256], replicated, may hold values from -3 to 3
- step_bias: float32 [128], P('head'), may hold values from -5 to -3
- log_rate: float32 [128], P('head'), may hold values from -6 to 4
Outputs:
- layer_output: bfloat16 [4096, 8192], P('seq', 'head')
Inputs may be any that keep to these rules, and one draw needn't show every extreme that they name: `doc_lengths`: the 16 documents lie one after another, their lengths sum to 4096, and the last one holds 2560 positions.
All inputs are finite; a program needn't handle non-finite values.
Results may differ from a plain program's by a relative error of at most 0.015.
Values may be sent and summed in bfloat16 or wider, within the bound.
A program may use at most 128 MiB of HBM per device.

v0:
```python
import functools

import jax
import jax.numpy as jnp
from jax import lax
from jax.experimental import pallas as pl
from jax.experimental.pallas import tpu as pltpu
from jax.sharding import PartitionSpec as P

HEADS = 128
GROUPS = 8
BLOCK = 256


def passed_along(value, axis, steps):
    count = lax.axis_size(axis)
    leading, last = (max(0, -steps), min(count, count - steps))
    return lax.ppermute(value, axis, [(source, source + steps) for source in range(leading, last)])


def segment_of(positions, starts):
    reached = (starts[None, :] <= positions[:, None]).astype(jnp.int32)
    return jnp.sum(reached, axis=1) - 1


def causal_conv(extended, taps_weight, seg_ext, row_count):
    tap_count = taps_weight.shape[0]
    own_segment = seg_ext[tap_count - 1 :]
    summed = jnp.zeros((row_count, extended.shape[1]), jnp.float32)
    for tap_index in range(tap_count):
        window = extended[tap_index : tap_index + row_count].astype(jnp.float32)
        keep_mask = (seg_ext[tap_index : tap_index + row_count] == own_segment).astype(jnp.float32)[
            :, None
        ]
        summed = summed + taps_weight[tap_index][None, :] * window * keep_mask
    return jax.nn.silu(summed).astype(jnp.bfloat16)


def block_terms(b_rows, c_rows, x_rows, decay_rows, step_rows, segments, seg_before):
    block_len = b_rows.shape[0]
    head_total = decay_rows.shape[0]
    x_heads = x_rows.reshape(block_len, head_total, -1)
    cumulative = jnp.cumsum(decay_rows, axis=1)
    products = jnp.dot(c_rows, b_rows.T, preferred_element_type=jnp.float32)
    local_index = jnp.arange(block_len)
    allowed = (local_index[None, :] <= local_index[:, None]) & (
        segments[None, :] == segments[:, None]
    )
    spread = cumulative[:, :, None] - cumulative[:, None, :]
    decay_mat = jnp.where(allowed[None], jnp.exp(jnp.where(allowed[None], spread, 0.0)), 0.0)
    scores = (products[None] * decay_mat * step_rows[:, None, :]).astype(jnp.bfloat16)
    y_inner = jnp.einsum("hij,jhp->ihp", scores, x_heads, preferred_element_type=jnp.float32)
    ending = cumulative[:, -1]
    trailing = (
        jnp.where((segments == segments[-1])[None, :], jnp.exp(ending[:, None] - cumulative), 0.0)
        * step_rows
    )
    weighted = (trailing.T[:, :, None] * x_heads.astype(jnp.float32)).astype(jnp.bfloat16)
    local_state = jnp.einsum("jn,jhp->hnp", b_rows, weighted, preferred_element_type=jnp.float32)
    factor = jnp.where(segments[-1] == seg_before, jnp.exp(ending), 0.0)
    entry_gain = jnp.where((segments == seg_before)[None, :], jnp.exp(cumulative), 0.0)
    return (y_inner.reshape(block_len, -1), local_state, factor, entry_gain)


def local_pass(state_cols, value_cols, decay_cols, step_cols, seg_rows, seg_before, block_len):
    block_count = state_cols.shape[0] // block_len
    state_dim = state_cols.shape[1] // 2
    head_total = decay_cols.shape[1]
    b_all = state_cols[:, :state_dim].reshape(block_count, block_len, state_dim)
    c_all = state_cols[:, state_dim:].reshape(block_count, block_len, state_dim)
    x_all = value_cols.reshape(block_count, block_len, -1)
    decay_all = decay_cols.reshape(block_count, block_len, head_total).transpose(0, 2, 1)
    step_all = step_cols.reshape(block_count, block_len, head_total).transpose(0, 2, 1)
    seg_all = seg_rows.reshape(block_count, block_len)

    def one_block(block_item):
        return block_terms(*block_item)

    outputs = lax.map(one_block, (b_all, c_all, x_all, decay_all, step_all, seg_all, seg_before))
    return (outputs, c_all)


def prefix_blocks(local_state, factor):

    def chain_step(carry_pair, block_item):
        running, running_gain = carry_pair
        local_term, factor_term = block_item
        return (
            (factor_term[:, None, None] * running + local_term, factor_term * running_gain),
            (running, running_gain),
        )

    initial = (
        jnp.zeros(local_state.shape[1:], jnp.float32),
        jnp.ones((factor.shape[1],), jnp.float32),
    )
    (shard_state, shard_gain), (inside, gain_list) = lax.scan(
        chain_step, initial, (local_state, factor)
    )
    return (shard_state, shard_gain, inside, gain_list)


def finish(y_inner, incoming, entry_gain, c_all, value_cols, gate_cols):
    block_count, block_len, _ = y_inner.shape
    head_total = incoming.shape[1]
    carried = jnp.einsum(
        "cin,chnp->cihp", c_all.astype(jnp.float32), incoming, precision=lax.Precision.HIGHEST
    )
    carried = carried * entry_gain.transpose(0, 2, 1)[:, :, :, None]
    x_heads = value_cols.reshape(block_count, block_len, head_total, -1).astype(jnp.float32)
    summed = y_inner.reshape(block_count, block_len, head_total, -1) + carried + x_heads
    gating = jax.nn.silu(gate_cols.astype(jnp.float32)).reshape(
        block_count, block_len, head_total, -1
    )
    return (summed * gating).reshape(block_count * block_len, -1).astype(jnp.bfloat16)


def local(
    tokens,
    doc_lengths,
    value_weight,
    gate_weight,
    state_weight,
    step_weight,
    value_conv,
    state_conv,
    step_bias,
    log_rate,
):
    tok_dev = tokens.shape[0] * lax.axis_size("head")
    heads_here = step_weight.shape[1]
    tap_count = value_conv.shape[0]
    group_index = lax.axis_index("head") * heads_here // (HEADS // GROUPS)
    state_own = lax.dynamic_index_in_dim(state_weight, group_index, 0, keepdims=False)
    conv_own = lax.dynamic_index_in_dim(state_conv, group_index, 0, keepdims=False)
    gathered = lax.all_gather(tokens, "head", axis=0, tiled=True)
    shard_pieces = (
        lax.all_gather(value_weight, "seq", axis=0, tiled=True),
        lax.all_gather(gate_weight, "seq", axis=0, tiled=True),
        lax.all_gather(state_own, "seq", axis=0, tiled=True),
        lax.all_gather(step_weight, "seq", axis=0, tiled=True),
    )
    projected = tuple(
        (
            jnp.dot(gathered, weight_piece, preferred_element_type=jnp.float32)
            for weight_piece in shard_pieces
        )
    )
    value_proj = projected[0].astype(jnp.bfloat16)
    gate_proj = projected[1].astype(jnp.bfloat16)
    state_proj = projected[2].astype(jnp.bfloat16)
    step_proj = projected[3].astype(jnp.bfloat16)
    value_cols = value_proj.shape[1]
    rim_source = jnp.concatenate(
        [value_proj[-(tap_count - 1) :], state_proj[-(tap_count - 1) :]], axis=1
    )
    rim_rows = passed_along(rim_source, "seq", 1)
    value_ext = jnp.concatenate([rim_rows[:, :value_cols], value_proj], axis=0)
    state_ext = jnp.concatenate([rim_rows[:, value_cols:], state_proj], axis=0)
    starts = jnp.cumsum(doc_lengths) - doc_lengths
    positions = lax.axis_index("seq") * tok_dev + jnp.arange(-(tap_count - 1), tok_dev)
    seg_ext = segment_of(positions, starts)
    value_act = causal_conv(value_ext, value_conv, seg_ext, tok_dev)
    state_act = causal_conv(state_ext, conv_own, seg_ext, tok_dev)
    step_size = jax.nn.softplus(step_proj.astype(jnp.float32) + step_bias[None, :])
    decay_rate = -jnp.exp(log_rate)[None, :] * step_size
    seg_rows = seg_ext[tap_count - 1 :]
    seg_before = seg_ext[tap_count - 2 : tap_count - 2 + tok_dev : BLOCK]
    (y_inner, local_state, factor, entry_gain), c_all = local_pass(
        state_act, value_act, decay_rate, step_size, seg_rows, seg_before, BLOCK
    )
    shard_state, shard_gain, inside, gain_list = prefix_blocks(local_state, factor)

    def relay(step_index, arriving):
        leaving = shard_gain[:, None, None] * arriving + shard_state
        return passed_along(leaving, "seq", 1)

    entering = lax.fori_loop(0, lax.axis_size("seq") - 1, relay, jnp.zeros_like(shard_state))
    incoming = inside + gain_list[:, :, None, None] * entering[None]
    return finish(y_inner, incoming, entry_gain, c_all, value_act, gate_proj)


MESH = pl.DeviceIdType.MESH
SEQ_FAST, HEAD_FAST = 4, 8
F32 = jnp.float32
BF16 = jnp.bfloat16


def spread_kernel(tok, value_w, gate_w, state_w, step_w, tok_all, w_all, step_all,
                  tok_send, tok_recv, wt_send, wt_recv, st_send, st_recv, own_sem):
    s = lax.axis_index("seq")
    h = lax.axis_index("head")
    y, x, c = h // 4, (h // 2) % 2, h % 2
    part = value_w.shape[0]
    cols = value_w.shape[1] // SEQ_FAST

    def head_of(yy, xx, cc):
        return yy * 4 + xx * 2 + cc

    mate, xnb, ynb = head_of(y, x, 1 - c), head_of(y, 1 - x, c), head_of(1 - y, x, c)
    barrier = pltpu.get_barrier_semaphore()
    for dist in range(1, SEQ_FAST):
        pl.semaphore_signal(barrier, inc=1, device_id=((s + dist) % SEQ_FAST, h), device_id_type=MESH)
    for nb in (mate, xnb, ynb):
        pl.semaphore_signal(barrier, inc=1, device_id=(s, nb), device_id_type=MESH)
    pl.semaphore_wait(barrier, SEQ_FAST + 2)

    def send(src, z, hh, to, kind):
        slot = z * HEAD_FAST + hh
        return pltpu.make_async_remote_copy(
            src_ref=src, dst_ref=tok_all.at[slot], send_sem=tok_send.at[kind, slot],
            recv_sem=tok_recv.at[slot], device_id=to, device_id_type=MESH)

    def arrived(z, hh):
        slot = z * HEAD_FAST + hh
        pltpu.make_async_remote_copy(
            src_ref=tok_all.at[slot], dst_ref=tok_all.at[slot], send_sem=tok_send.at[0, slot],
            recv_sem=tok_recv.at[slot], device_id=(s, mate), device_id_type=MESH).wait_recv()

    UP, DOWN, TOX, TOY, TOMATE = range(5)
    own = pltpu.make_async_copy(tok, tok_all.at[s * HEAD_FAST + h], own_sem.at[0])
    own.start()

    def plane(src, z):
        send(src, z, h, (s, xnb), TOX).start()
        send(src, z, h, (s, ynb), TOY).start()
        send(src, z, h, (s, mate), TOMATE).start()

    @pl.when(s < SEQ_FAST - 1)
    def _():
        send(tok, s, h, (s + 1, h), UP).start()

    @pl.when(s > 0)
    def _():
        send(tok, s, h, (s - 1, h), DOWN).start()

    plane(tok, s)

    def weights(dist):
        peer = (s + dist) % SEQ_FAST
        copies = []
        for which, ref in enumerate((value_w, gate_w)):
            src = ref.at[:, pl.ds(pl.multiple_of(peer * cols, cols), cols)]
            dst = w_all.at[pl.ds(pl.multiple_of(s * part, part), part), pl.ds(which * cols, cols)]
            copies.append((src, dst, which))
        copies.append((step_w.at[peer], step_all.at[:, pl.ds(pl.multiple_of(s * part, part), part)], 2))
        if dist == 0:
            copies.append((state_w.at[h], w_all.at[pl.ds(pl.multiple_of(s * part, part), part), pl.ds(2 * cols, state_w.shape[2])], 3))
            return [pltpu.make_async_copy(src, dst, own_sem.at[1 + which]) for src, dst, which in copies]
        return [pltpu.make_async_remote_copy(
            src_ref=src, dst_ref=dst, send_sem=wt_send.at[dist, which], recv_sem=wt_recv.at[dist, which],
            device_id=(peer, h), device_id_type=MESH) for src, dst, which in copies]

    own_weights = weights(0)
    for copy in own_weights:
        copy.start()

    def state_send(src, z, to, way):
        return pltpu.make_async_remote_copy(
            src_ref=src, dst_ref=w_all.at[pl.ds(pl.multiple_of(z * part, part), part), pl.ds(2 * cols, state_w.shape[2])],
            send_sem=st_send.at[way, z], recv_sem=st_recv.at[z], device_id=to, device_id_type=MESH)

    def state_piece(z):
        return w_all.at[pl.ds(pl.multiple_of(z * part, part), part), pl.ds(2 * cols, state_w.shape[2])]

    def both_sides(dist, act):
        @pl.when(s - dist >= 0)
        def _():
            act(s - dist, s < SEQ_FAST - 1, s + 1, UP)

        if dist > 0:
            @pl.when(s + dist < SEQ_FAST)
            def _():
                act(s + dist, s > 0, s - 1, DOWN)

    def token_round(z, onward, nxt, way):
        arrived(z, h)
        block = tok_all.at[z * HEAD_FAST + h]

        @pl.when(onward)
        def _():
            send(block, z, h, (nxt, h), way).start()

        plane(block, z)

    def state_round(z, onward, nxt, way):
        state_send(state_piece(z), z, (nxt, h), way).wait_recv()

        @pl.when(onward)
        def _():
            state_send(state_piece(z), z, (nxt, h), way).start()

    def relay(z, hh, to, kind):
        slot = z * HEAD_FAST + hh
        send(tok_all.at[slot], z, hh, to, kind).start()

    def plane_round(z, onward, nxt, way):
        arrived(z, xnb)

        @pl.when(z % 2 == 0)
        def _():
            relay(z, xnb, (s, ynb), TOY)

        relay(z, xnb, (s, mate), TOMATE)
        arrived(z, ynb)

        @pl.when(z % 2 == 1)
        def _():
            relay(z, ynb, (s, xnb), TOX)

        relay(z, ynb, (s, mate), TOMATE)

    both_sides(1, token_round)

    @pl.when(s < SEQ_FAST - 1)
    def _():
        state_send(state_w.at[h], s, (s + 1, h), UP).start()

    @pl.when(s > 0)
    def _():
        state_send(state_w.at[h], s, (s - 1, h), DOWN).start()

    both_sides(0, plane_round)
    both_sides(2, token_round)
    peer_weights = [weights(dist) for dist in range(1, SEQ_FAST)]
    for which in range(3):
        for copies in peer_weights:
            copies[which].start()
    both_sides(1, state_round)
    both_sides(1, plane_round)
    both_sides(3, token_round)
    both_sides(2, state_round)
    both_sides(2, plane_round)
    both_sides(3, state_round)
    both_sides(3, plane_round)
    diag = head_of(1 - y, 1 - x, c)
    for dist in range(SEQ_FAST):
        z = (s + dist) % SEQ_FAST
        arrived(z, diag)
        relay(z, diag, (s, mate), TOMATE)
    for dist in range(SEQ_FAST):
        z = (s + dist) % SEQ_FAST
        for yy, xx in ((y, x), (y, 1 - x), (1 - y, x), (1 - y, 1 - x)):
            arrived(z, head_of(yy, xx, 1 - c))

    for copies in peer_weights:
        for copy in copies:
            copy.wait()
    own.wait()
    for copy in own_weights:
        copy.wait()

    def sent(z, hh, kind):
        send(tok_all.at[z * HEAD_FAST + hh], z, hh, (s, mate), kind).wait_send()

    for z in range(SEQ_FAST):
        @pl.when((z <= s) & (s < SEQ_FAST - 1))
        def _():
            sent(z, h, UP)
            state_send(state_piece(z), z, (s, mate), UP).wait_send()

        @pl.when((z >= s) & (s > 0))
        def _():
            sent(z, h, DOWN)
            state_send(state_piece(z), z, (s, mate), DOWN).wait_send()

    for dist in range(SEQ_FAST):
        z = (s + dist) % SEQ_FAST
        sent(z, h, TOX)
        sent(z, h, TOY)
        for hh in (h, xnb, ynb, diag):
            sent(z, hh, TOMATE)

        @pl.when(z % 2 == 0)
        def _():
            sent(z, xnb, TOY)

        @pl.when(z % 2 == 1)
        def _():
            sent(z, ynb, TOX)


def spread(tokens, value_weight, gate_weight, state_weight, step_parts):
    rows, width = tokens.shape
    part, wide = value_weight.shape
    cols = wide // SEQ_FAST
    any_spec = pl.BlockSpec(memory_space=pl.ANY)
    count = SEQ_FAST * HEAD_FAST
    return pl.pallas_call(
        spread_kernel,
        out_shape=(
            jax.ShapeDtypeStruct((count, rows, width), BF16),
            jax.ShapeDtypeStruct((part * SEQ_FAST, 2 * cols + state_weight.shape[2]), BF16),
            jax.ShapeDtypeStruct((step_parts.shape[1], part * SEQ_FAST), BF16),
        ),
        in_specs=[any_spec] * 5,
        out_specs=(any_spec,) * 3,
        scratch_shapes=[
            pltpu.SemaphoreType.DMA((5, count)),
            pltpu.SemaphoreType.DMA((count,)),
            pltpu.SemaphoreType.DMA((SEQ_FAST, 3)),
            pltpu.SemaphoreType.DMA((SEQ_FAST, 3)),
            pltpu.SemaphoreType.DMA((2, SEQ_FAST)),
            pltpu.SemaphoreType.DMA((SEQ_FAST,)),
            pltpu.SemaphoreType.DMA((5,)),
        ],
        compiler_params=pltpu.CompilerParams(collective_id=0, has_side_effects=True),
        name="spread",
    )(tokens, value_weight, gate_weight, state_weight, step_parts)


def fast_dot(left, right, dims=((1,), (0,))):
    return lax.dot_general(left, right, (dims, ((), ())), preferred_element_type=F32)


def silu(value):
    return value * lax.logistic(value)


def parts_of(value):
    high = value.astype(BF16)
    rest = value - high.astype(F32)
    mid = rest.astype(BF16)
    return high, mid, (rest - mid.astype(F32)).astype(BF16)


def project(tokens, w_all, step_all, proj_to, step_to):
    proj_to[...] = fast_dot(tokens, w_all[...]).astype(BF16)
    step_to[...] = fast_dot(tokens, step_all[...], ((1,), (1,))).astype(BF16).astype(F32)


def one_block(heads_here, cols, proj, step_proj, segments, seg_row, seg_before, taps, bias, rate, carry, state):
    block_len = proj.shape[0]
    chan = cols // heads_here
    state_dim = (proj.shape[1] - 2 * cols) // 2
    tap_count = taps.shape[0]
    gate = proj[:, cols:2 * cols].astype(F32)
    conv_in = jnp.concatenate([proj[:, :cols], proj[:, 2 * cols:]], axis=1).astype(F32)
    tail = carry[...]
    carry[...] = conv_in[block_len - 8:]
    extended = jnp.concatenate([tail, conv_in], axis=0)
    summed = conv_in * taps[tap_count - 1:tap_count, :]
    for back in range(1, tap_count):
        window = extended[8 - back:8 - back + block_len]
        keep = segments[:, back:back + 1] > 0
        summed = summed + jnp.where(keep, taps[tap_count - 1 - back:tap_count - back, :] * window, 0.0)
    act = silu(summed).astype(BF16)
    x = act[:, :cols]
    b_rows = act[:, cols:cols + state_dim]
    c_rows = act[:, cols + state_dim:]

    raw = step_proj + bias
    step = jnp.maximum(raw, 0.0) + jnp.log1p(jnp.exp(-jnp.abs(raw)))
    width = step.shape[1]
    decay = -jnp.exp(rate) * step
    row_id = lax.broadcasted_iota(jnp.int32, (block_len, block_len), 0)
    col_id = lax.broadcasted_iota(jnp.int32, (block_len, block_len), 1)
    lower = col_id <= row_id
    sums = fast_dot(lower.astype(F32).astype(BF16), jnp.concatenate(parts_of(decay), axis=1))
    cum = sums[:, :width] + sums[:, width:2 * width] + sums[:, 2 * width:]
    turned = jnp.concatenate([cum, step], axis=1).T
    cum_t, step_t = turned[:width], turned[width:]
    allowed = lower & (seg_row == segments[:, 0:1])
    products = jnp.where(allowed, fast_dot(c_rows, b_rows, ((1,), (1,))), 0.0)
    head_of_col = lax.broadcasted_iota(jnp.int32, (block_len, cols), 1) // chan
    xf = x.astype(F32)
    scores, x_parts = [], []
    for head in range(heads_here):
        spread_ij = jnp.where(lower, cum[:, head:head + 1] - cum_t[head:head + 1, :], 0.0)
        scores.append((products * jnp.exp(spread_ij) * step_t[head:head + 1, :]).astype(BF16))
        x_parts.append(jnp.where(head_of_col == head, xf, 0.0).astype(BF16))
    inner = fast_dot(jnp.concatenate(scores, axis=1), jnp.concatenate(x_parts, axis=0))

    last = segments[block_len - 1:block_len, 0:1]
    ending = cum[block_len - 1:block_len, :]
    trailing = jnp.where(segments[:, 0:1] == last, jnp.exp(ending - cum), 0.0) * step
    gain = jnp.where(segments[:, 0:1] == seg_before, jnp.exp(cum), 0.0)
    pick_row = lax.broadcasted_iota(jnp.int32, (6 * width, 2 * cols), 0)
    pick_col = lax.broadcasted_iota(jnp.int32, (6 * width, 2 * cols), 1)
    pick = ((pick_row % width == (pick_col % cols) // chan)
            & (pick_row // (3 * width) == pick_col // cols)).astype(F32).astype(BF16)
    wide = fast_dot(jnp.concatenate(parts_of(trailing) + parts_of(gain), axis=1), pick)
    weighted = (wide[:, :cols] * xf).astype(BF16)
    gain_cols = wide[:, cols:]
    entering = state[...]
    high, mid, _ = parts_of(entering)
    carried = fast_dot(jnp.concatenate([c_rows, c_rows], axis=1), jnp.concatenate([high, mid], axis=0))
    state[...] = gain_cols[block_len - 1:block_len, :] * entering + fast_dot(b_rows, weighted, ((0,), (0,)))
    total = inner + gain_cols * carried + xf
    return (total * silu(gate)).astype(BF16)


def layer_kernel(heads_here, block_len, tok, w_all, step_all, seg_col_odd, seg_col_even, seg_row_odd, seg_row_even,
                 before_odd, before_even, taps, bias, rate, out,
                 carry, state, proj_even, step_even, proj_odd, step_odd, stage, send_sem, recv_sem, own_sem):
    step_id = pl.program_id(0)
    steps = pl.num_programs(0) - 1
    count = stage.shape[0]
    cols = stage.shape[2]
    per_peer = count // SEQ_FAST
    s = lax.axis_index("seq")
    h = lax.axis_index("head")

    def sending(block):
        return pltpu.make_async_remote_copy(
            src_ref=stage.at[block],
            dst_ref=out.at[pl.ds(pl.multiple_of((block % per_peer) * block_len, block_len), block_len),
                           pl.ds(pl.multiple_of(s * cols, cols), cols)],
            send_sem=send_sem.at[block], recv_sem=recv_sem.at[s, block % per_peer],
            device_id=(block // per_peer, h), device_id_type=MESH)

    def keeping(block):
        return pltpu.make_async_copy(
            stage.at[block],
            out.at[pl.ds(pl.multiple_of((block % per_peer) * block_len, block_len), block_len),
                   pl.ds(pl.multiple_of(s * cols, cols), cols)], own_sem.at[block % per_peer])

    def ship(block):
        @pl.when(block // per_peer != s)
        def _():
            sending(block).start()

        @pl.when(block // per_peer == s)
        def _():
            keeping(block).start()

    @pl.when(step_id == 0)
    def _():
        barrier = pltpu.get_barrier_semaphore()
        for dist in range(1, SEQ_FAST):
            pl.semaphore_signal(barrier, inc=1, device_id=((s + dist) % SEQ_FAST, h), device_id_type=MESH)
        pl.semaphore_wait(barrier, SEQ_FAST - 1)
        carry[...] = jnp.zeros_like(carry)
        state[...] = jnp.zeros_like(state)
        proj_odd[...] = jnp.zeros_like(proj_odd)
        step_odd[...] = jnp.zeros_like(step_odd)

    odd = jnp.maximum(2 * step_id - 1, 0)
    project(tok[:block_len], w_all, step_all, proj_even, step_even)
    stage[odd] = one_block(heads_here, cols, proj_odd[...], step_odd[...], seg_col_odd[...], seg_row_odd[0],
                           before_odd[0][:, 0:1], taps[...], bias[...], rate[...], carry, state)

    @pl.when(step_id > 0)
    def _():
        ship(2 * step_id - 1)

    @pl.when(step_id < steps)
    def _():
        project(tok[block_len:], w_all, step_all, proj_odd, step_odd)
        stage[2 * step_id] = one_block(
            heads_here, cols, proj_even[...], step_even[...], seg_col_even[...], seg_row_even[0],
            before_even[0][:, 0:1], taps[...], bias[...], rate[...], carry, state)
        ship(2 * step_id)

    @pl.when(step_id == steps)
    def _():
        for block in range(count):
            @pl.when(block // per_peer != s)
            def _():
                sending(block).wait_send()

            @pl.when(block // per_peer == s)
            def _():
                keeping(block).wait()

        for dist in range(1, SEQ_FAST):
            peer = (s + dist) % SEQ_FAST
            for index in range(per_peer):
                rows = pl.ds(index * block_len, block_len)
                there = out.at[rows, pl.ds(pl.multiple_of(peer * cols, cols), cols)]
                pltpu.make_async_remote_copy(
                    src_ref=there, dst_ref=there, send_sem=send_sem.at[0], recv_sem=recv_sem.at[peer, index],
                    device_id=(peer, h), device_id_type=MESH).wait_recv()


def layer(tok_all, w_all, step_all, seg_col, seg_row, before, taps, bias, rate, cols, heads_here, block_len):
    count = tok_all.shape[0] // block_len
    steps = count // 2
    fixed = lambda array: pl.BlockSpec(array.shape, lambda i: (0,) * array.ndim)
    odd = lambda i: jnp.maximum(2 * i - 1, 0)
    even = lambda i: jnp.minimum(2 * i, count - 2)
    return pl.pallas_call(
        functools.partial(layer_kernel, heads_here, block_len),
        grid=(steps + 1,),
        out_shape=jax.ShapeDtypeStruct((tok_all.shape[0] // SEQ_FAST, cols * SEQ_FAST), BF16),
        in_specs=[
            pl.BlockSpec((2 * block_len, tok_all.shape[1]), lambda i: (jnp.minimum(i, steps - 1), 0)),
            fixed(w_all), fixed(step_all),
            pl.BlockSpec((block_len, seg_col.shape[1]), lambda i: (odd(i), 0)),
            pl.BlockSpec((block_len, seg_col.shape[1]), lambda i: (even(i), 0)),
            pl.BlockSpec((1, 1, block_len), lambda i: (odd(i), 0, 0)),
            pl.BlockSpec((1, 1, block_len), lambda i: (even(i), 0, 0)),
            pl.BlockSpec((1, 1, before.shape[2]), lambda i: (odd(i), 0, 0)),
            pl.BlockSpec((1, 1, before.shape[2]), lambda i: (even(i), 0, 0)),
            fixed(taps), fixed(bias), fixed(rate),
        ],
        out_specs=pl.BlockSpec(memory_space=pl.ANY),
        scratch_shapes=[
            pltpu.VMEM((8, taps.shape[1]), F32),
            pltpu.VMEM(((w_all.shape[1] - 2 * cols) // 2, cols), F32),
            pltpu.VMEM((block_len, w_all.shape[1]), BF16),
            pltpu.VMEM((block_len, step_all.shape[0]), F32),
            pltpu.VMEM((block_len, w_all.shape[1]), BF16),
            pltpu.VMEM((block_len, step_all.shape[0]), F32),
            pltpu.VMEM((count, block_len, cols), BF16),
            pltpu.SemaphoreType.DMA((count,)),
            pltpu.SemaphoreType.DMA((SEQ_FAST, count // SEQ_FAST)),
            pltpu.SemaphoreType.DMA((count // SEQ_FAST,)),
        ],
        compiler_params=pltpu.CompilerParams(
            collective_id=1, has_side_effects=True, vmem_limit_bytes=56 * 1024 * 1024),
        name="layer",
    )(tok_all, w_all, step_all, seg_col, seg_col, seg_row, seg_row, before, before, taps, bias, rate)


def prepared(doc_lengths, value_conv, state_conv, step_bias, log_rate, total, cols, heads_here):
    s = lax.axis_index("seq")
    tap_count = value_conv.shape[0]
    conv_own = lax.dynamic_index_in_dim(state_conv, lax.axis_index("head"), 0, keepdims=False)
    taps = jnp.concatenate([lax.dynamic_slice_in_dim(value_conv, s * cols, cols, 1), conv_own], axis=1)
    starts = jnp.cumsum(doc_lengths) - doc_lengths
    seg_ext = segment_of(jnp.arange(-(tap_count - 1), total), starts)
    seg_rows = seg_ext[tap_count - 1:]
    same = [(seg_ext[tap_count - 1 - back:tap_count - 1 - back + total] == seg_rows).astype(jnp.int32)
            for back in range(1, tap_count)]
    seg_col = jnp.stack([seg_rows] + same, axis=1)
    seg_row = seg_rows.reshape(-1, 1, BLOCK)
    before = jnp.broadcast_to(seg_ext[tap_count - 2:tap_count - 2 + total:BLOCK][:, None, None],
                              (total // BLOCK, 1, 128))
    bias = lax.dynamic_slice_in_dim(step_bias, s * heads_here, heads_here, 0)
    rate = lax.dynamic_slice_in_dim(log_rate, s * heads_here, heads_here, 0)
    pad = (0, STEP_ROWS - heads_here)
    return taps, seg_col, seg_row, before, jnp.pad(bias, pad)[None], jnp.pad(rate, pad)[None]


STEP_ROWS = 16


def local_fast(tokens, doc_lengths, value_weight, gate_weight, state_weight, step_weight,
               value_conv, state_conv, step_bias, log_rate):
    total = tokens.shape[0] * SEQ_FAST * HEAD_FAST
    cols = value_weight.shape[1] // SEQ_FAST
    heads_here = step_weight.shape[1] // SEQ_FAST
    step_parts = step_weight.T.reshape(SEQ_FAST, heads_here, -1)
    step_parts = jnp.pad(step_parts, ((0, 0), (0, STEP_ROWS - heads_here), (0, 0)))
    small = prepared(doc_lengths, value_conv, state_conv, step_bias, log_rate, total, cols, heads_here)
    tok_all, w_all, step_all = spread(tokens, value_weight, gate_weight, state_weight, step_parts)
    taps, seg_col, seg_row, before, bias, rate = small
    return layer(tok_all.reshape(total, -1), w_all, step_all, seg_col, seg_row, before, taps, bias, rate,
                 cols, heads_here, BLOCK)


def solution(mesh):
    fast = mesh.shape["seq"] == SEQ_FAST and mesh.shape["head"] == HEAD_FAST
    return jax.shard_map(
        local_fast if fast else local,
        mesh=mesh,
        in_specs=(
            P(("seq", "head"), None),
            P(),
            P("seq", "head"),
            P("seq", "head"),
            P(None, "seq", None),
            P("seq", "head"),
            P(None, "head"),
            P(),
            P("head"),
            P("head"),
        ),
        out_specs=P("seq", "head"),
        check_vma=False,
    )
```

profile of v0, /device:TPU:24, one launch (start us, length us, event | category | flops | bytes accessed | tf_op | source)
XLA Modules:
  0.0 310.7 jit_solution(13925433749549597223)
XLA Ops:
  0.0 0.0 copy-start
  0.0 0.7 dynamic_slice.15
  0.7 0.7 dynamic_slice.16
  1.5 0.6 pad_bitcast_fusion
  2.1 0.7 constant_dynamic-slice_fusion
  2.7 0.0 copy-done
  2.7 0.6 pad_maximum_fusion.taps
  3.3 0.7 copy.20
  4.1 0.1 reduce
  4.2 0.7 sub.7
  4.9 0.1 convert_reduce_fusion
  5.0 0.1 slice.19
  5.1 0.7 broadcast_in_dim.6.before_odd.before_even
  5.8 0.1 slice.20
  5.9 0.0 copy-start.1
  5.9 0.1 fusion
  6.0 0.1 pad_add_fusion
  6.1 0.8 reshape.43
  6.8 0.7 pad.11.step_w
  7.5 2.0 copy.21.seg_col_odd.seg_col_even
  9.5 207.3 %spread.1 = (bf16[32,128,4096]{2,1,0:T(8,128)(2,1)}, bf16[4096,768]{1,0:T(8,128)(2,1)}, bf16[16,4096]{1,0:T(8,128)(2,1)}) custom-call(bf16[128,4096]{1,0:T(8,128)(2,1)} %tok.1, bf16[1024,1024]{1,0:T(8,128)(2,1)} %value_w.1, bf16[1024,1024]{1,0:T(8,128)(2,1)} %gate_w.1, bf16[8,1024,256]{2,1,0:T(8,128)(2,1)} %state_w.1, bf16[4,16,1024]{2,1,0:T(8,128)(2,1)} %pad.11.step_w), custom_call_target="tpu_custom_call" | custom-call | tf_op jit(solution)/shard_map/spread/pallas_call | solution.py:389
  216.7 0.0 copy-done.1
  216.7 90.9 %layer.1 = bf16[1024,1024]{1,0:T(8,128)(2,1)} custom-call(bf16[4096,4096]{1,0:T(8,128)(2,1)} %bitcast.14, bf16[4096,768]{1,0:T(8,128)(2,1)} %get-tuple-element.9.w_all, bf16[16,4096]{1,0:T(8,128)(2,1)} %get-tuple-element.10.step_all, s32[4096,4]{1,0:T(8,128)} %copy.21.seg_col_odd.seg_col_even, s32[4096,4]{1,0:T(8,128)} %copy.21.seg_col_odd.seg_col_even, ...), custom_call_target="tpu_custom_call" | custom-call | tf_op jit(solution)/shard_map/layer/pallas_call | solution.py:582
  307.7 3.1 copy.24
  (4 shorter events, 0.0 us)
Async XLA Ops:
  0.0 2.7 copy-start
  5.9 210.8 %copy-start.1 = (s32[4096]{0:T(1024)}, s32[4096]{0:T(1024)S(1)}, u32[]{:S(2)}) copy-start(s32[4096]{0:T(1024)S(1)} %slice.20) | copy-start | bytes 49156
where the time goes:
time: 311 us
  Pallas kernels  298 us (96%)
  local copies, waits for them, and re-layouts  10.8 us (3%)
    pallas_call x1, Pallas kernels, spread(): pl.pallas_call(spread_kernel, out_shape=(jax.ShapeDtypeStruct((count, row...  207 us
    pallas_call x1, Pallas kernels, layer(): pl.pallas_call(functools.partial(layer_kernel, heads_here, block_len), gr...  90.9 us

commit v1 on v0

--- a/solution.py
+++ b/solution.py
@@ -2,6 +2,7 @@
 
 import jax
 import jax.numpy as jnp
+import numpy as np
 from jax import lax
 from jax.experimental import pallas as pl
 from jax.experimental.pallas import tpu as pltpu
@@ -186,8 +187,8 @@
 BF16 = jnp.bfloat16
 
 
-def spread_kernel(tok, value_w, gate_w, state_w, step_w, tok_all, w_all, step_all,
-                  tok_send, tok_recv, wt_send, wt_recv, st_send, st_recv, own_sem):
+def spread_kernel(tok, value_w, gate_w, state_w, step_w, tok_all, w_vs, w_gate, step_all, proj, step_proj,
+                  tok_send, tok_recv, wt_send, wt_recv, st_send, st_recv, own_sem, vs_here, step_here, fetch_sem):
     s = lax.axis_index("seq")
     h = lax.axis_index("head")
     y, x, c = h // 4, (h // 2) % 2, h % 2
@@ -241,11 +242,11 @@
         copies = []
         for which, ref in enumerate((value_w, gate_w)):
             src = ref.at[:, pl.ds(pl.multiple_of(peer * cols, cols), cols)]
-            dst = w_all.at[pl.ds(pl.multiple_of(s * part, part), part), pl.ds(which * cols, cols)]
+            dst = (w_vs, w_gate)[which].at[pl.ds(pl.multiple_of(s * part, part), part), pl.ds(0, cols)]
             copies.append((src, dst, which))
         copies.append((step_w.at[peer], step_all.at[:, pl.ds(pl.multiple_of(s * part, part), part)], 2))
         if dist == 0:
-            copies.append((state_w.at[h], w_all.at[pl.ds(pl.multiple_of(s * part, part), part), pl.ds(2 * cols, state_w.shape[2])], 3))
+            copies.append((state_w.at[h], w_vs.at[pl.ds(pl.multiple_of(s * part, part), part), pl.ds(cols, state_w.shape[2])], 3))
             return [pltpu.make_async_copy(src, dst, own_sem.at[1 + which]) for src, dst, which in copies]
         return [pltpu.make_async_remote_copy(
             src_ref=src, dst_ref=dst, send_sem=wt_send.at[dist, which], recv_sem=wt_recv.at[dist, which],
@@ -255,13 +256,16 @@
     for copy in own_weights:
         copy.start()
 
+    def sent(z, hh, kind):
+        send(tok_all.at[z * HEAD_FAST + hh], z, hh, (s, mate), kind).wait_send()
+
     def state_send(src, z, to, way):
         return pltpu.make_async_remote_copy(
-            src_ref=src, dst_ref=w_all.at[pl.ds(pl.multiple_of(z * part, part), part), pl.ds(2 * cols, state_w.shape[2])],
+            src_ref=src, dst_ref=w_vs.at[pl.ds(pl.multiple_of(z * part, part), part), pl.ds(cols, state_w.shape[2])],
             send_sem=st_send.at[way, z], recv_sem=st_recv.at[z], device_id=to, device_id_type=MESH)
 
     def state_piece(z):
-        return w_all.at[pl.ds(pl.multiple_of(z * part, part), part), pl.ds(2 * cols, state_w.shape[2])]
+        return w_vs.at[pl.ds(pl.multiple_of(z * part, part), part), pl.ds(cols, state_w.shape[2])]
 
     def both_sides(dist, act):
         @pl.when(s - dist >= 0)
@@ -310,29 +314,38 @@
 
         relay(z, ynb, (s, mate), TOMATE)
 
+    def token_left(z, onward, nxt, way):
+        @pl.when(onward)
+        def _():
+            sent(z, h, way)
+
     both_sides(1, token_round)
-
-    @pl.when(s < SEQ_FAST - 1)
-    def _():
-        state_send(state_w.at[h], s, (s + 1, h), UP).start()
-
-    @pl.when(s > 0)
-    def _():
-        state_send(state_w.at[h], s, (s - 1, h), DOWN).start()
-
     both_sides(0, plane_round)
     both_sides(2, token_round)
-    peer_weights = [weights(dist) for dist in range(1, SEQ_FAST)]
-    for which in range(3):
-        for copies in peer_weights:
-            copies[which].start()
-    both_sides(1, state_round)
+
+    @pl.when(s < SEQ_FAST - 1)
+    def _():
+        state_send(state_w.at[h], s, (s + 1, h), UP).start()
+
+    @pl.when(s > 0)
+    def _():
+        state_send(state_w.at[h], s, (s - 1, h), DOWN).start()
+
     both_sides(1, plane_round)
     both_sides(3, token_round)
+    both_sides(1, state_round)
+    both_sides(2, token_left)
+    peer_weights = [weights(dist) for dist in range(1, SEQ_FAST)]
+    for copies in peer_weights:
+        copies[0].start()
+        copies[2].start()
+    both_sides(2, plane_round)
     both_sides(2, state_round)
-    both_sides(2, plane_round)
-    both_sides(3, state_round)
     both_sides(3, plane_round)
+    for copies in peer_weights:
+        copies[0].wait_send()
+    for copies in peer_weights:
+        copies[1].start()
     diag = head_of(1 - y, 1 - x, c)
     for dist in range(SEQ_FAST):
         z = (s + dist) % SEQ_FAST
@@ -343,27 +356,54 @@
         for yy, xx in ((y, x), (y, 1 - x), (1 - y, x), (1 - y, 1 - x)):
             arrived(z, head_of(yy, xx, 1 - c))
 
-    for copies in peer_weights:
-        for copy in copies:
-            copy.wait()
+    both_sides(3, state_round)
     own.wait()
     for copy in own_weights:
         copy.wait()
-
-    def sent(z, hh, kind):
-        send(tok_all.at[z * HEAD_FAST + hh], z, hh, (s, mate), kind).wait_send()
+    for copies in peer_weights:
+        copies[0].wait_recv()
+        copies[2].wait()
+    fetches = [pltpu.make_async_copy(w_vs, vs_here, fetch_sem.at[0]),
+               pltpu.make_async_copy(step_all, step_here, fetch_sem.at[1])]
+    for copy in fetches:
+        copy.start()
+    for copy in fetches:
+        copy.wait()
+
+    def project(tokens, proj_to, step_to):
+        rows = tokens[...].reshape(-1, tokens.shape[2])
+        proj_to[...] = fast_dot(rows, vs_here[...]).astype(BF16)
+        step_to[...] = fast_dot(rows, step_here[...], ((1,), (1,))).astype(BF16).astype(F32)
+
+    count, rows, width = tok_all.shape
+    pltpu.emit_pipeline(
+        project, grid=(count // 2,),
+        in_specs=[pl.BlockSpec((2, rows, width), lambda i: (i, 0, 0))],
+        out_specs=[pl.BlockSpec((2 * rows, proj.shape[1]), lambda i: (i, 0)),
+                   pl.BlockSpec((2 * rows, step_proj.shape[1]), lambda i: (i, 0))],
+    )(tok_all, proj, step_proj)
+    for copies in peer_weights:
+        copies[1].wait()
 
     for z in range(SEQ_FAST):
         @pl.when((z <= s) & (s < SEQ_FAST - 1))
         def _():
-            sent(z, h, UP)
             state_send(state_piece(z), z, (s, mate), UP).wait_send()
 
         @pl.when((z >= s) & (s > 0))
         def _():
-            sent(z, h, DOWN)
             state_send(state_piece(z), z, (s, mate), DOWN).wait_send()
 
+    @pl.when(s < SEQ_FAST - 1)
+    def _():
+        sent(s, h, UP)
+
+    @pl.when(s > 0)
+    def _():
+        sent(s, h, DOWN)
+
+    both_sides(1, token_left)
+    both_sides(3, token_left)
     for dist in range(SEQ_FAST):
         z = (s + dist) % SEQ_FAST
         sent(z, h, TOX)
@@ -390,11 +430,14 @@
         spread_kernel,
         out_shape=(
             jax.ShapeDtypeStruct((count, rows, width), BF16),
-            jax.ShapeDtypeStruct((part * SEQ_FAST, 2 * cols + state_weight.shape[2]), BF16),
+            jax.ShapeDtypeStruct((part * SEQ_FAST, cols + state_weight.shape[2]), BF16),
+            jax.ShapeDtypeStruct((part * SEQ_FAST, cols), BF16),
             jax.ShapeDtypeStruct((step_parts.shape[1], part * SEQ_FAST), BF16),
+            jax.ShapeDtypeStruct((count * rows, cols + state_weight.shape[2]), BF16),
+            jax.ShapeDtypeStruct((count * rows, step_parts.shape[1]), F32),
         ),
         in_specs=[any_spec] * 5,
-        out_specs=(any_spec,) * 3,
+        out_specs=(any_spec,) * 6,
         scratch_shapes=[
             pltpu.SemaphoreType.DMA((5, count)),
             pltpu.SemaphoreType.DMA((count,)),
@@ -403,8 +446,12 @@
             pltpu.SemaphoreType.DMA((2, SEQ_FAST)),
             pltpu.SemaphoreType.DMA((SEQ_FAST,)),
             pltpu.SemaphoreType.DMA((5,)),
+            pltpu.VMEM((part * SEQ_FAST, cols + state_weight.shape[2]), BF16),
+            pltpu.VMEM((step_parts.shape[1], part * SEQ_FAST), BF16),
+            pltpu.SemaphoreType.DMA((2,)),
         ],
-        compiler_params=pltpu.CompilerParams(collective_id=0, has_side_effects=True),
+        compiler_params=pltpu.CompilerParams(
+            collective_id=0, has_side_effects=True, vmem_limit_bytes=32 * 1024 * 1024),
         name="spread",
     )(tokens, value_weight, gate_weight, state_weight, step_parts)
 
@@ -424,25 +471,21 @@
     return high, mid, (rest - mid.astype(F32)).astype(BF16)
 
 
-def project(tokens, w_all, step_all, proj_to, step_to):
-    proj_to[...] = fast_dot(tokens, w_all[...]).astype(BF16)
-    step_to[...] = fast_dot(tokens, step_all[...], ((1,), (1,))).astype(BF16).astype(F32)
-
-
-def one_block(heads_here, cols, proj, step_proj, segments, seg_row, seg_before, taps, bias, rate, carry, state):
+def one_block(heads_here, cols, proj, step_proj, gate, segments, seg_row, taps, bias, rate, pick, carry, state):
     block_len = proj.shape[0]
+    half = block_len // 2
     chan = cols // heads_here
-    state_dim = (proj.shape[1] - 2 * cols) // 2
+    state_dim = (proj.shape[1] - cols) // 2
     tap_count = taps.shape[0]
-    gate = proj[:, cols:2 * cols].astype(F32)
-    conv_in = jnp.concatenate([proj[:, :cols], proj[:, 2 * cols:]], axis=1).astype(F32)
+    conv_in = proj.astype(F32)
     tail = carry[...]
     carry[...] = conv_in[block_len - 8:]
     extended = jnp.concatenate([tail, conv_in], axis=0)
     summed = conv_in * taps[tap_count - 1:tap_count, :]
+    own = segments[:, 0:1]
     for back in range(1, tap_count):
         window = extended[8 - back:8 - back + block_len]
-        keep = segments[:, back:back + 1] > 0
+        keep = segments[:, back:back + 1] == own
         summed = summed + jnp.where(keep, taps[tap_count - 1 - back:tap_count - back, :] * window, 0.0)
     act = silu(summed).astype(BF16)
     x = act[:, :cols]
@@ -460,25 +503,25 @@
     cum = sums[:, :width] + sums[:, width:2 * width] + sums[:, 2 * width:]
     turned = jnp.concatenate([cum, step], axis=1).T
     cum_t, step_t = turned[:width], turned[width:]
-    allowed = lower & (seg_row == segments[:, 0:1])
+    allowed = lower & (seg_row == own)
     products = jnp.where(allowed, fast_dot(c_rows, b_rows, ((1,), (1,))), 0.0)
-    head_of_col = lax.broadcasted_iota(jnp.int32, (block_len, cols), 1) // chan
+    head_of_col = lax.broadcasted_iota(jnp.int32, (1, cols), 1) // chan
     xf = x.astype(F32)
-    scores, x_parts = [], []
-    for head in range(heads_here):
-        spread_ij = jnp.where(lower, cum[:, head:head + 1] - cum_t[head:head + 1, :], 0.0)
-        scores.append((products * jnp.exp(spread_ij) * step_t[head:head + 1, :]).astype(BF16))
-        x_parts.append(jnp.where(head_of_col == head, xf, 0.0).astype(BF16))
-    inner = fast_dot(jnp.concatenate(scores, axis=1), jnp.concatenate(x_parts, axis=0))
-
-    last = segments[block_len - 1:block_len, 0:1]
+    x_parts = [jnp.where(head_of_col == head, xf, 0.0).astype(BF16) for head in range(heads_here)]
+
+    def rows_of(first, rows, upto):
+        scores = []
+        for head in range(heads_here):
+            spread_ij = jnp.minimum(cum[first:first + rows, head:head + 1] - cum_t[head:head + 1, :upto], 0.0)
+            scores.append((products[first:first + rows, :upto] * jnp.exp(spread_ij)
+                           * step_t[head:head + 1, :upto]).astype(BF16))
+        return fast_dot(jnp.concatenate(scores, axis=1), jnp.concatenate([xp[:upto] for xp in x_parts], axis=0))
+
+    inner = jnp.concatenate([rows_of(0, half, half), rows_of(half, half, block_len)], axis=0)
+
     ending = cum[block_len - 1:block_len, :]
-    trailing = jnp.where(segments[:, 0:1] == last, jnp.exp(ending - cum), 0.0) * step
-    gain = jnp.where(segments[:, 0:1] == seg_before, jnp.exp(cum), 0.0)
-    pick_row = lax.broadcasted_iota(jnp.int32, (6 * width, 2 * cols), 0)
-    pick_col = lax.broadcasted_iota(jnp.int32, (6 * width, 2 * cols), 1)
-    pick = ((pick_row % width == (pick_col % cols) // chan)
-            & (pick_row // (3 * width) == pick_col // cols)).astype(F32).astype(BF16)
+    trailing = jnp.where(own == own[block_len - 1:block_len], jnp.exp(ending - cum), 0.0) * step
+    gain = jnp.where(own == segments[0:1, 1:2], jnp.exp(cum), 0.0)
     wide = fast_dot(jnp.concatenate(parts_of(trailing) + parts_of(gain), axis=1), pick)
     weighted = (wide[:, :cols] * xf).astype(BF16)
     gain_cols = wide[:, cols:]
@@ -490,41 +533,30 @@
     return (total * silu(gate)).astype(BF16)
 
 
-def layer_kernel(heads_here, block_len, tok, w_all, step_all, seg_col_odd, seg_col_even, seg_row_odd, seg_row_even,
-                 before_odd, before_even, taps, bias, rate, out,
-                 carry, state, proj_even, step_even, proj_odd, step_odd, stage, send_sem, recv_sem, own_sem):
-    step_id = pl.program_id(0)
-    steps = pl.num_programs(0) - 1
+def layer_kernel(heads_here, tok, w_gate, proj, step_proj, segs, value_taps, state_taps, head_terms, pick, out,
+                 carry, state, stage, send_sem, recv_sem, own_sem):
+    block = pl.program_id(0)
     count = stage.shape[0]
-    cols = stage.shape[2]
+    block_len, cols = stage.shape[1:]
     per_peer = count // SEQ_FAST
     s = lax.axis_index("seq")
     h = lax.axis_index("head")
 
-    def sending(block):
+    def sending(index):
         return pltpu.make_async_remote_copy(
-            src_ref=stage.at[block],
-            dst_ref=out.at[pl.ds(pl.multiple_of((block % per_peer) * block_len, block_len), block_len),
+            src_ref=stage.at[index],
+            dst_ref=out.at[pl.ds(pl.multiple_of((index % per_peer) * block_len, block_len), block_len),
                            pl.ds(pl.multiple_of(s * cols, cols), cols)],
-            send_sem=send_sem.at[block], recv_sem=recv_sem.at[s, block % per_peer],
-            device_id=(block // per_peer, h), device_id_type=MESH)
-
-    def keeping(block):
+            send_sem=send_sem.at[index], recv_sem=recv_sem.at[s, index % per_peer],
+            device_id=(index // per_peer, h), device_id_type=MESH)
+
+    def keeping(index):
         return pltpu.make_async_copy(
-            stage.at[block],
-            out.at[pl.ds(pl.multiple_of((block % per_peer) * block_len, block_len), block_len),
-                   pl.ds(pl.multiple_of(s * cols, cols), cols)], own_sem.at[block % per_peer])
-
-    def ship(block):
-        @pl.when(block // per_peer != s)
-        def _():
-            sending(block).start()
-
-        @pl.when(block // per_peer == s)
-        def _():
-            keeping(block).start()
-
-    @pl.when(step_id == 0)
+            stage.at[index],
+            out.at[pl.ds(pl.multiple_of((index % per_peer) * block_len, block_len), block_len),
+                   pl.ds(pl.multiple_of(s * cols, cols), cols)], own_sem.at[index % per_peer])
+
+    @pl.when(block == 0)
     def _():
         barrier = pltpu.get_barrier_semaphore()
         for dist in range(1, SEQ_FAST):
@@ -532,105 +564,79 @@
         pl.semaphore_wait(barrier, SEQ_FAST - 1)
         carry[...] = jnp.zeros_like(carry)
         state[...] = jnp.zeros_like(state)
-        proj_odd[...] = jnp.zeros_like(proj_odd)
-        step_odd[...] = jnp.zeros_like(step_odd)
-
-    odd = jnp.maximum(2 * step_id - 1, 0)
-    project(tok[:block_len], w_all, step_all, proj_even, step_even)
-    stage[odd] = one_block(heads_here, cols, proj_odd[...], step_odd[...], seg_col_odd[...], seg_row_odd[0],
-                           before_odd[0][:, 0:1], taps[...], bias[...], rate[...], carry, state)
-
-    @pl.when(step_id > 0)
-    def _():
-        ship(2 * step_id - 1)
-
-    @pl.when(step_id < steps)
-    def _():
-        project(tok[block_len:], w_all, step_all, proj_odd, step_odd)
-        stage[2 * step_id] = one_block(
-            heads_here, cols, proj_even[...], step_even[...], seg_col_even[...], seg_row_even[0],
-            before_even[0][:, 0:1], taps[...], bias[...], rate[...], carry, state)
-        ship(2 * step_id)
-
-    @pl.when(step_id == steps)
-    def _():
-        for block in range(count):
-            @pl.when(block // per_peer != s)
+
+    gate = fast_dot(tok[...], w_gate[...]).astype(BF16).astype(F32)
+    taps = jnp.concatenate([value_taps[:, pl.ds(pl.multiple_of(s * cols, cols), cols)], state_taps[h]], axis=1)
+    stage[block] = one_block(heads_here, cols, proj[...], step_proj[...], gate, segs[...].T, segs[0:1, :],
+                             taps, head_terms[0:1, :], head_terms[1:2, :], pick[...], carry, state)
+
+    @pl.when(block // per_peer != s)
+    def _():
+        sending(block).start()
+
+    @pl.when(block // per_peer == s)
+    def _():
+        keeping(block).start()
+
+    @pl.when(block == count - 1)
+    def _():
+        for index in range(count):
+            @pl.when(index // per_peer != s)
             def _():
-                sending(block).wait_send()
-
-            @pl.when(block // per_peer == s)
+                sending(index).wait_send()
+
+            @pl.when(index // per_peer == s)
             def _():
-                keeping(block).wait()
+                keeping(index).wait()
 
         for dist in range(1, SEQ_FAST):
             peer = (s + dist) % SEQ_FAST
             for index in range(per_peer):
-                rows = pl.ds(index * block_len, block_len)
-                there = out.at[rows, pl.ds(pl.multiple_of(peer * cols, cols), cols)]
+                there = out.at[pl.ds(index * block_len, block_len), pl.ds(pl.multiple_of(peer * cols, cols), cols)]
                 pltpu.make_async_remote_copy(
                     src_ref=there, dst_ref=there, send_sem=send_sem.at[0], recv_sem=recv_sem.at[peer, index],
                     device_id=(peer, h), device_id_type=MESH).wait_recv()
 
 
-def layer(tok_all, w_all, step_all, seg_col, seg_row, before, taps, bias, rate, cols, heads_here, block_len):
+def layer(tok_all, w_gate, proj, step_proj, segs, value_taps, state_taps, head_terms, pick, heads_here, block_len):
     count = tok_all.shape[0] // block_len
-    steps = count // 2
+    cols = w_gate.shape[1]
     fixed = lambda array: pl.BlockSpec(array.shape, lambda i: (0,) * array.ndim)
-    odd = lambda i: jnp.maximum(2 * i - 1, 0)
-    even = lambda i: jnp.minimum(2 * i, count - 2)
+    by_rows = lambda array: pl.BlockSpec((block_len, array.shape[1]), lambda i: (i, 0))
     return pl.pallas_call(
-        functools.partial(layer_kernel, heads_here, block_len),
-        grid=(steps + 1,),
+        functools.partial(layer_kernel, heads_here),
+        grid=(count,),
         out_shape=jax.ShapeDtypeStruct((tok_all.shape[0] // SEQ_FAST, cols * SEQ_FAST), BF16),
         in_specs=[
-            pl.BlockSpec((2 * block_len, tok_all.shape[1]), lambda i: (jnp.minimum(i, steps - 1), 0)),
-            fixed(w_all), fixed(step_all),
-            pl.BlockSpec((block_len, seg_col.shape[1]), lambda i: (odd(i), 0)),
-            pl.BlockSpec((block_len, seg_col.shape[1]), lambda i: (even(i), 0)),
-            pl.BlockSpec((1, 1, block_len), lambda i: (odd(i), 0, 0)),
-            pl.BlockSpec((1, 1, block_len), lambda i: (even(i), 0, 0)),
-            pl.BlockSpec((1, 1, before.shape[2]), lambda i: (odd(i), 0, 0)),
-            pl.BlockSpec((1, 1, before.shape[2]), lambda i: (even(i), 0, 0)),
-            fixed(taps), fixed(bias), fixed(rate),
+            by_rows(tok_all), fixed(w_gate), by_rows(proj), by_rows(step_proj),
+            pl.BlockSpec((segs.shape[0], block_len), lambda i: (0, i)),
+            fixed(value_taps), fixed(state_taps), fixed(head_terms), fixed(pick),
         ],
         out_specs=pl.BlockSpec(memory_space=pl.ANY),
         scratch_shapes=[
-            pltpu.VMEM((8, taps.shape[1]), F32),
-            pltpu.VMEM(((w_all.shape[1] - 2 * cols) // 2, cols), F32),
-            pltpu.VMEM((block_len, w_all.shape[1]), BF16),
-            pltpu.VMEM((block_len, step_all.shape[0]), F32),
-            pltpu.VMEM((block_len, w_all.shape[1]), BF16),
-            pltpu.VMEM((block_len, step_all.shape[0]), F32),
+            pltpu.VMEM((8, proj.shape[1]), F32),
+            pltpu.VMEM(((proj.shape[1] - cols) // 2, cols), F32),
             pltpu.VMEM((count, block_len, cols), BF16),
             pltpu.SemaphoreType.DMA((count,)),
             pltpu.SemaphoreType.DMA((SEQ_FAST, count // SEQ_FAST)),
             pltpu.SemaphoreType.DMA((count // SEQ_FAST,)),
         ],
         compiler_params=pltpu.CompilerParams(
-            collective_id=1, has_side_effects=True, vmem_limit_bytes=56 * 1024 * 1024),
+            collective_id=1, has_side_effects=True, vmem_limit_bytes=48 * 1024 * 1024),
         name="layer",
-    )(tok_all, w_all, step_all, seg_col, seg_col, seg_row, seg_row, before, before, taps, bias, rate)
-
-
-def prepared(doc_lengths, value_conv, state_conv, step_bias, log_rate, total, cols, heads_here):
+    )(tok_all, w_gate, proj, step_proj, segs, value_taps, state_taps, head_terms, pick)
+
+
+def prepared(doc_lengths, step_bias, log_rate, total, cols, heads_here):
     s = lax.axis_index("seq")
-    tap_count = value_conv.shape[0]
-    conv_own = lax.dynamic_index_in_dim(state_conv, lax.axis_index("head"), 0, keepdims=False)
-    taps = jnp.concatenate([lax.dynamic_slice_in_dim(value_conv, s * cols, cols, 1), conv_own], axis=1)
     starts = jnp.cumsum(doc_lengths) - doc_lengths
-    seg_ext = segment_of(jnp.arange(-(tap_count - 1), total), starts)
-    seg_rows = seg_ext[tap_count - 1:]
-    same = [(seg_ext[tap_count - 1 - back:tap_count - 1 - back + total] == seg_rows).astype(jnp.int32)
-            for back in range(1, tap_count)]
-    seg_col = jnp.stack([seg_rows] + same, axis=1)
-    seg_row = seg_rows.reshape(-1, 1, BLOCK)
-    before = jnp.broadcast_to(seg_ext[tap_count - 2:tap_count - 2 + total:BLOCK][:, None, None],
-                              (total // BLOCK, 1, 128))
-    bias = lax.dynamic_slice_in_dim(step_bias, s * heads_here, heads_here, 0)
-    rate = lax.dynamic_slice_in_dim(log_rate, s * heads_here, heads_here, 0)
-    pad = (0, STEP_ROWS - heads_here)
-    return taps, seg_col, seg_row, before, jnp.pad(bias, pad)[None], jnp.pad(rate, pad)[None]
+    at = jnp.arange(total)[None, :] - jnp.arange(8)[:, None]
+    segs = (jnp.sum((starts[:, None, None] <= at[None]).astype(jnp.int32), axis=0) - 1).astype(F32)
+    terms = lax.dynamic_slice_in_dim(jnp.stack([step_bias, log_rate]), s * heads_here, heads_here, 1)
+    head_terms = jnp.pad(terms, ((0, 0), (0, STEP_ROWS - heads_here)))
+    row, col = np.arange(6 * STEP_ROWS)[:, None], np.arange(2 * cols)[None, :]
+    pick = (row % STEP_ROWS == (col % cols) // (cols // heads_here)) & (row // (3 * STEP_ROWS) == col // cols)
+    return segs, head_terms, jnp.asarray(pick, BF16)
 
 
 STEP_ROWS = 16
@@ -643,11 +649,10 @@
     heads_here = step_weight.shape[1] // SEQ_FAST
     step_parts = step_weight.T.reshape(SEQ_FAST, heads_here, -1)
     step_parts = jnp.pad(step_parts, ((0, 0), (0, STEP_ROWS - heads_here), (0, 0)))
-    small = prepared(doc_lengths, value_conv, state_conv, step_bias, log_rate, total, cols, heads_here)
-    tok_all, w_all, step_all = spread(tokens, value_weight, gate_weight, state_weight, step_parts)
-    taps, seg_col, seg_row, before, bias, rate = small
-    return layer(tok_all.reshape(total, -1), w_all, step_all, seg_col, seg_row, before, taps, bias, rate,
-                 cols, heads_here, BLOCK)
+    segs, head_terms, pick = prepared(doc_lengths, step_bias, log_rate, total, cols, heads_here)
+    tok_all, _, w_gate, _, proj, step_proj = spread(tokens, value_weight, gate_weight, state_weight, step_parts)
+    return layer(tok_all.reshape(total, -1), w_gate, proj, step_proj, segs, value_conv, state_conv, head_terms,
+                 pick, heads_here, BLOCK)
 
 
 def solution(mesh):

time: 311 us -> 282 us (0.907)
  Pallas kernels: 298 us -> 269 us
    pallas_call x1, Pallas kernels: 90.9 us -> 75.4 us  [layer(): pl.pallas_call(functools.partial(layer_kernel, heads_here), grid=(count,)...]
    pallas_call x1, Pallas kernels: 207 us -> 194 us  [spread(): pl.pallas_call(spread_kernel, out_shape=(jax.ShapeDtypeStruct((count, row...]
    unnamed x5 -> x25, local copies, waits for them, and re-layouts: 3.09 us -> 11.3 us
where the time goes in v1:
time: 282 us
  Pallas kernels  269 us (95%)
  local copies, waits for them, and re-layouts  12.3 us (4%)
    pallas_call x1, Pallas kernels, spread(): pl.pallas_call(spread_kernel, out_shape=(jax.ShapeDtypeStruct((count, row...  194 us
    pallas_call x1, Pallas kernels, layer(): pl.pallas_call(functools.partial(layer_kernel, heads_here), grid=(count,)...  75.4 us
    unnamed x25, local copies, waits for them, and re-layouts  11.3 us

profile of v1, /device:TPU:24, one launch (start us, length us, event | category | flops | bytes accessed | tf_op | source)
XLA Modules:
  0.0 281.9 jit_solution(8891386509356615292)
XLA Ops:
  0.0 0.8 reshape.45
  0.8 0.0 copy-start.1
  0.8 2.2 copy-done.1
  3.0 1.6 copy-done.3
  4.6 1.6 copy-done.4
  6.2 1.2 copy-done.5
  7.4 0.0 copy-start.7
  7.4 0.0 copy-start.8
  7.4 193.6 %spread.1 = (bf16[32,128,4096]{2,1,0:T(8,128)(2,1)}, bf16[4096,512]{1,0:T(8,128)(2,1)}, bf16[4096,256]{1,0:T(8,128)(2,1)S(1)}, bf16[16,4096]{1,0:T(8,128)(2,1)},...) custom-call(bf16[128,4096]{1,0:T(8,128)(2,1)S(1)} %copy-done.5, bf16[1024,1024]{1,0:T(8,128)(2,1)S(1)} %copy-done.3, ...), custom_call_target="tpu_custom_call" | custom-call | tf_op jit(solution)/shard_map/spread/pallas_call | solution.py:429
  201.0 0.0 copy-start
  201.0 2.0 copy-done
  203.1 1.3 copy-done.2
  204.4 0.0 copy-done.9
  204.4 0.1 copy.14
  204.6 0.1 reduce
  204.7 0.3 convert_reduce_fusion
  205.0 0.0 copy-done.10
  205.0 0.0 copy-done.11
  205.0 0.1 constant_dynamic-slice_fusion
  205.1 0.0 copy-done.6
  205.1 0.0 copy-done.7
  205.1 0.0 copy-done.8
  205.1 75.4 %layer.1 = bf16[1024,1024]{1,0:T(8,128)(2,1)S(1)} custom-call(bf16[4096,4096]{1,0:T(8,128)(2,1)} %bitcast.5, bf16[4096,256]{1,0:T(8,128)(2,1)S(1)} %get-tuple-element.10.w_gate, bf16[4096,512]{1,0:T(8,128)(2,1)} %copy-done, f32[4096,16]{1,0:T(8,128)} %copy-done.2, f32[8,4096]{1,0:T(8,128)S(1)} %add_convert_fusion.segs, f32[4,1024]{1,0:T(4,128)S(1)} %copy-done.8, ...), custom_call_target="tpu_custom_call" | custom-call | tf_op jit(solution)/shard_map/layer/pallas_call | solution.py:606
  280.5 1.3 copy.16
  (15 shorter events, 0.1 us)
Async XLA Ops:
  0.8 2.2 copy-start.1
  3.0 1.6 copy-start.3
  4.6 1.6 copy-start.4
  6.2 1.2 copy-start.5
  7.4 197.0 %copy-start.9 = (s32[16]{0:T(128)S(1)}, s32[16]{0:T(128)}, u32[]{:S(2)}) copy-start(s32[16]{0:T(128)} %param.12) | copy-start | bytes 196
  7.4 197.6 %copy-start.10 = (f32[16]{0:T(128)S(1)}, f32[16]{0:T(128)}, u32[]{:S(2)}) copy-start(f32[16]{0:T(128)} %param.20) | copy-start | bytes 196
  7.4 197.6 %copy-start.11 = (f32[16]{0:T(128)S(1)}, f32[16]{0:T(128)}, u32[]{:S(2)}) copy-start(f32[16]{0:T(128)} %param.19) | copy-start | bytes 196
  7.4 197.7 %copy-start.6 = (bf16[96,512]{1,0:T(8,128)(2,1)S(1)}, bf16[96,512]{1,0:T(8,128)(2,1)}, u32[]{:S(2)}) copy-start(bf16[96,512]{1,0:T(8,128)(2,1)} %constant.23.clone.pick) | copy-start | bytes 294916
  7.4 197.7 %copy-start.7 = (f32[8,4,256]{2,1,0:T(4,128)S(1)}, f32[8,4,256]{2,1,0:T(4,128)}, u32[]{:S(2)}) copy-start(f32[8,4,256]{2,1,0:T(4,128)} %state_taps.1) | copy-start | bytes 98308
  7.4 197.7 %copy-start.8 = (f32[4,1024]{1,0:T(4,128)S(1)}, f32[4,1024]{1,0:T(4,128)}, u32[]{:S(2)}) copy-start(f32[4,1024]{1,0:T(4,128)} %value_taps.1) | copy-start | bytes 49156
  201.0 2.1 copy-start
  203.1 1.3 copy-start.2
